TPU v7x, 32 devices: a whole 2x2x4 slice. The times are simulated.
32 devices in a mesh: leaf: 32 (over z, y, x, core).
Axes of the slice: x: 2, y: 2, z: 4, core: 2. Of those that a mesh axis runs over, the one named last changes fastest.
Arguments:
- right_sides: bfloat16 [64, 32768], P(None, 'leaf'), may hold values from -6 to 6
- leaf_inverse: bfloat16 [32768, 1024], P('leaf'), may hold values from -0.1875 to 0.1875
- leaf_basis: bfloat16 [32768, 256], P('leaf'), may hold values from -0.1875 to 0.1875
- transfer: bfloat16 [16384, 256], P('leaf'), may hold values from -0.25 to 0.25
- coupling: bfloat16 [16384, 256], P('leaf'), may hold values from -0.25 to 0.25
Outputs:
- solution: bfloat16 [64, 32768], P(None, 'leaf')
All inputs are finite; a program needn't handle non-finite values.
Results may differ from a plain program's by a relative error of at most 0.025.
Values may be sent and summed in bfloat16 or wider, within the bound.
A program may use at most 64 MiB of HBM per device.

v0:
```python
import jax
import jax.numpy as jnp
from jax import lax
from jax.sharding import PartitionSpec as P


def from_partner(block, axis, bit):
    count = lax.axis_size(axis)
    route = []
    for low in range(count):
        high = low | 1 << bit
        if high != low and high < count:
            route += [(low, high), (high, low)]
    return lax.ppermute(block, axis, route)


def times_matrix(values, matrix):
    return jnp.dot(values, matrix, preferred_element_type=jnp.float32)


def times_transposed(values, matrix):
    return lax.dot_general(
        values, matrix, (((1,), (1,)), ((), ())), preferred_element_type=jnp.float32
    )


def body(right_sides, leaf_inverse, leaf_basis, transfer, coupling):
    levels = lax.axis_size("leaf").bit_length() - 1
    rank_width = leaf_basis.shape[1]
    own_map = transfer[:rank_width]
    other_map = transfer[rank_width:]
    from_other = coupling[:rank_width]
    from_own = coupling[rank_width:]
    current = times_matrix(right_sides, leaf_basis).astype(jnp.bfloat16)
    own_values = []
    far_values = []
    for tree_level in range(1, levels + 1):
        other = from_partner(current, "leaf", tree_level - 1)
        own_values.append(current)
        far_values.append(other)
        current = (times_matrix(current, own_map) + times_matrix(other, other_map)).astype(
            jnp.bfloat16
        )
    node_h = current
    for tree_level in range(levels, 0, -1):
        own_t = own_values[tree_level - 1]
        other_h, far_t = from_partner((node_h, own_t), "leaf", tree_level - 1)
        total = times_transposed(node_h, own_map) + times_transposed(other_h, other_map)
        total = total + times_matrix(far_t, from_other)
        total = total + times_matrix(own_t, from_own)
        node_h = total.astype(jnp.bfloat16)
    total = times_matrix(right_sides, leaf_inverse) + times_transposed(node_h, leaf_basis)
    return total.astype(jnp.bfloat16)


def solution(mesh):
    placed = (P(None, "leaf"), P("leaf", None), P("leaf", None), P("leaf", None), P("leaf", None))
    return jax.shard_map(
        body, mesh=mesh, in_specs=placed, out_specs=P(None, "leaf"), check_vma=False
    )
```

profile of v0, /device:TPU:1, one launch (start us, length us, event | category | flops | bytes accessed | tf_op | source)
XLA Modules:
  0.0 43.3 jit_solution(3974802743340974666)
XLA Ops:
  0.0 1.5 %convolution_convert_fusion = bf16[64,256]{1,0:T(8,128)(2,1)S(1)} fusion(bf16[64,1024]{1,0:T(8,128)(2,1)} %param.5, bf16[1024,256]{1,0:T(8,128)(2,1)} %param.7), kind=kOutput, calls=%fused_computation.32 | convolution fusion | flops 33570816 | bytes 688128 | tf_op jit(solution)/shard_map/dot_general | solution.py:18
  1.6 1.0 %fusion.60 = f32[64,256]{1,0:T(8,128)S(1)} fusion(bf16[64,256]{1,0:T(8,128)(2,1)S(1)} %convolution_convert_fusion, bf16[512,256]{1,0:T(8,128)(2,1)} %param.8), kind=kOutput, calls=%fused_computation.76 | convolution fusion | flops 8388608 | bytes 229376 | tf_op jit(solution)/shard_map/dot_general | solution.py:18
  2.6 1.4 %fusion.62 = f32[64,1024]{1,0:T(8,128)S(1)} fusion(bf16[64,1024]{1,0:T(8,128)(2,1)} %param.5, bf16[1024,1024]{1,0:T(8,128)(2,1)S(1)} %copy-done), kind=kOutput, calls=%fused_computation.78 | convolution fusion | flops 134217728 | bytes 2490368 | tf_op jit(solution)/shard_map/dot_general | solution.py:18
  4.4 2.7 %collective-permute-start.1 = (bf16[64,256]{1,0:T(8,128)(2,1)S(1)}, bf16[64,256]{1,0:T(8,128)(2,1)S(1)}, u32[]{:S(2)}, u32[]{:S(2)}) collective-permute-start(bf16[64,256]{1,0:T(8,128)(2,1)S(1)} %fusion.6), channel_id=1, source_target_pairs={{0,2},{2,0},{1,3},{3,1},{4,6},{6,4},{5,7},{7,5},{8,10},{10,8},{9,1... | collective-permute-start | bytes 98312 | tf_op jit(solution)/shard_map/ppermute | solution.py:14
  7.2 0.2 fusion.18
  7.3 1.5 %collective-permute-done.1 = bf16[64,256]{1,0:T(8,128)(2,1)S(1)} collective-permute-done((bf16[64,256]{1,0:T(8,128)(2,1)S(1)}, bf16[64,256]{1,0:T(8,128)(2,1)S(1)}, u32[]{:S(2)}, u32[]{:S(2)}) %collective-permute-start.1) | collective-permute-done | bytes 32800 | tf_op jit(solution)/shard_map/ppermute | solution.py:14
  8.9 1.1 %collective-permute-start.2 = (bf16[64,256]{1,0:T(8,128)(2,1)S(1)}, bf16[64,256]{1,0:T(8,128)(2,1)S(1)}, u32[]{:S(2)}, u32[]{:S(2)}) collective-permute-start(bf16[64,256]{1,0:T(8,128)(2,1)S(1)} %fusion.7), channel_id=1, source_target_pairs={{0,4},{4,0},{1,5},{5,1},{2,6},{6,2},{3,7},{7,3},{8,12},{12,8},{9,1... | collective-permute-start | bytes 98312 | tf_op jit(solution)/shard_map/ppermute | solution.py:14
  10.1 0.2 fusion.20
  10.3 1.4 %collective-permute-done.2 = bf16[64,256]{1,0:T(8,128)(2,1)S(1)} collective-permute-done((bf16[64,256]{1,0:T(8,128)(2,1)S(1)}, bf16[64,256]{1,0:T(8,128)(2,1)S(1)}, u32[]{:S(2)}, u32[]{:S(2)}) %collective-permute-start.2) | collective-permute-done | bytes 32800 | tf_op jit(solution)/shard_map/ppermute | solution.py:14
  11.9 1.1 %collective-permute-start.3 = (bf16[64,256]{1,0:T(8,128)(2,1)S(1)}, bf16[64,256]{1,0:T(8,128)(2,1)S(1)}, u32[]{:S(2)}, u32[]{:S(2)}) collective-permute-start(bf16[64,256]{1,0:T(8,128)(2,1)S(1)} %fusion.8), channel_id=1, source_target_pairs={{0,8},{8,0},{1,9},{9,1},{2,10},{10,2},{3,11},{11,3},{4,12},{12,4},... | collective-permute-start | bytes 98312 | tf_op jit(solution)/shard_map/ppermute | solution.py:14
  13.1 0.2 fusion.22
  13.3 1.4 %collective-permute-done.3 = bf16[64,256]{1,0:T(8,128)(2,1)S(1)} collective-permute-done((bf16[64,256]{1,0:T(8,128)(2,1)S(1)}, bf16[64,256]{1,0:T(8,128)(2,1)S(1)}, u32[]{:S(2)}, u32[]{:S(2)}) %collective-permute-start.3) | collective-permute-done | bytes 32800 | tf_op jit(solution)/shard_map/ppermute | solution.py:14
  14.8 0.2 fusion.52
  14.9 2.1 %collective-permute-start.4 = (bf16[64,256]{1,0:T(8,128)(2,1)S(1)}, bf16[64,256]{1,0:T(8,128)(2,1)S(1)}, u32[]{:S(2)}, u32[]{:S(2)}) collective-permute-start(bf16[64,256]{1,0:T(8,128)(2,1)S(1)} %fusion.9), channel_id=1, source_target_pairs={{0,16},{16,0},{1,17},{17,1},{2,18},{18,2},{3,19},{19,3},{4,20},{20... | collective-permute-start | bytes 98312 | tf_op jit(solution)/shard_map/ppermute | solution.py:14
  17.2 1.4 %collective-permute-done.4 = bf16[64,256]{1,0:T(8,128)(2,1)S(1)} collective-permute-done((bf16[64,256]{1,0:T(8,128)(2,1)S(1)}, bf16[64,256]{1,0:T(8,128)(2,1)S(1)}, u32[]{:S(2)}, u32[]{:S(2)}) %collective-permute-start.4) | collective-permute-done | bytes 32800 | tf_op jit(solution)/shard_map/ppermute | solution.py:14
  18.8 2.2 %collective-permute-start.5 = (bf16[64,256]{1,0:T(8,128)(2,1)S(1)}, bf16[64,256]{1,0:T(8,128)(2,1)S(1)}, u32[]{:S(2)}, u32[]{:S(2)}) collective-permute-start(bf16[64,256]{1,0:T(8,128)(2,1)S(1)} %fusion.10), channel_id=1, source_target_pairs={{0,16},{16,0},{1,17},{17,1},{2,18},{18,2},{3,19},{19,3},{4,20},{20... | collective-permute-start | bytes 98312 | tf_op jit(solution)/shard_map/ppermute | solution.py:14
  21.1 1.5 %collective-permute-done.5 = bf16[64,256]{1,0:T(8,128)(2,1)S(1)} collective-permute-done((bf16[64,256]{1,0:T(8,128)(2,1)S(1)}, bf16[64,256]{1,0:T(8,128)(2,1)S(1)}, u32[]{:S(2)}, u32[]{:S(2)}) %collective-permute-start.5) | collective-permute-done | bytes 32800 | tf_op jit(solution)/shard_map/ppermute | solution.py:14
  22.6 0.2 convolution_add_fusion.10
  22.7 0.2 fusion.11
  22.9 1.7 %collective-permute-start.6 = (bf16[64,256]{1,0:T(8,128)(2,1)S(1)}, bf16[64,256]{1,0:T(8,128)(2,1)S(1)}, u32[]{:S(2)}, u32[]{:S(2)}) collective-permute-start(bf16[64,256]{1,0:T(8,128)(2,1)S(1)} %fusion.11), channel_id=1, source_target_pairs={{0,8},{8,0},{1,9},{9,1},{2,10},{10,2},{3,11},{11,3},{4,12},{12,4},... | collective-permute-start | bytes 98312 | tf_op jit(solution)/shard_map/ppermute | solution.py:14
  24.7 1.2 %collective-permute-done.6 = bf16[64,256]{1,0:T(8,128)(2,1)S(1)} collective-permute-done((bf16[64,256]{1,0:T(8,128)(2,1)S(1)}, bf16[64,256]{1,0:T(8,128)(2,1)S(1)}, u32[]{:S(2)}, u32[]{:S(2)}) %collective-permute-start.6) | collective-permute-done | bytes 32800 | tf_op jit(solution)/shard_map/ppermute | solution.py:14
  26.0 0.2 fusion.12
  26.2 1.3 %collective-permute-start.7 = (bf16[64,256]{1,0:T(8,128)(2,1)S(1)}, bf16[64,256]{1,0:T(8,128)(2,1)S(1)}, u32[]{:S(2)}, u32[]{:S(2)}) collective-permute-start(bf16[64,256]{1,0:T(8,128)(2,1)S(1)} %fusion.12), channel_id=1, source_target_pairs={{0,4},{4,0},{1,5},{5,1},{2,6},{6,2},{3,7},{7,3},{8,12},{12,8},{9,1... | collective-permute-start | bytes 98312 | tf_op jit(solution)/shard_map/ppermute | solution.py:14
  27.7 1.3 %collective-permute-done.7 = bf16[64,256]{1,0:T(8,128)(2,1)S(1)} collective-permute-done((bf16[64,256]{1,0:T(8,128)(2,1)S(1)}, bf16[64,256]{1,0:T(8,128)(2,1)S(1)}, u32[]{:S(2)}, u32[]{:S(2)}) %collective-permute-start.7) | collective-permute-done | bytes 32800 | tf_op jit(solution)/shard_map/ppermute | solution.py:14
  29.1 0.2 fusion.13
  29.3 1.3 %collective-permute-start.8 = (bf16[64,256]{1,0:T(8,128)(2,1)S(1)}, bf16[64,256]{1,0:T(8,128)(2,1)S(1)}, u32[]{:S(2)}, u32[]{:S(2)}) collective-permute-start(bf16[64,256]{1,0:T(8,128)(2,1)S(1)} %fusion.13), channel_id=1, source_target_pairs={{0,2},{2,0},{1,3},{3,1},{4,6},{6,4},{5,7},{7,5},{8,10},{10,8},{9,1... | collective-permute-start | bytes 98312 | tf_op jit(solution)/shard_map/ppermute | solution.py:14
  30.8 1.4 %collective-permute-done.8 = bf16[64,256]{1,0:T(8,128)(2,1)S(1)} collective-permute-done((bf16[64,256]{1,0:T(8,128)(2,1)S(1)}, bf16[64,256]{1,0:T(8,128)(2,1)S(1)}, u32[]{:S(2)}, u32[]{:S(2)}) %collective-permute-start.8) | collective-permute-done | bytes 32800 | tf_op jit(solution)/shard_map/ppermute | solution.py:14
  32.1 0.2 convolution_add_fusion.4
  32.3 0.2 fusion.14
  32.5 8.8 %collective-permute-start.9 = (bf16[64,256]{1,0:T(8,128)(2,1)S(1)}, bf16[64,256]{1,0:T(8,128)(2,1)S(1)}, u32[]{:S(2)}, u32[]{:S(2)}) collective-permute-start(bf16[64,256]{1,0:T(8,128)(2,1)S(1)} %fusion.14), channel_id=1, source_target_pairs={{0,1},{1,0},{2,3},{3,2},{4,5},{5,4},{6,7},{7,6},{8,9},{9,8},{10,11... | collective-permute-start | bytes 98312 | tf_op jit(solution)/shard_map/ppermute | solution.py:14
  41.4 0.7 %collective-permute-done.9 = bf16[64,256]{1,0:T(8,128)(2,1)S(1)} collective-permute-done((bf16[64,256]{1,0:T(8,128)(2,1)S(1)}, bf16[64,256]{1,0:T(8,128)(2,1)S(1)}, u32[]{:S(2)}, u32[]{:S(2)}) %collective-permute-start.9) | collective-permute-done | bytes 32800 | tf_op jit(solution)/shard_map/ppermute | solution.py:14
  42.3 1.0 %fusion = bf16[64,1024]{1,0:T(8,128)(2,1)} fusion(f32[64,1024]{1,0:T(8,128)S(1)} %fusion.62, bf16[1024,256]{1,0:T(8,128)(2,1)S(1)} %copy-done.3, f32[64,256]{1,0:T(8,128)S(1)} %fusion.16, f32[64,256]{1,0:T(8,128)S(1)} %convolution_add_fusion.2, bf16[64,256]{1,0:T(8,128)(2,1)S(1)} %collective-permute-done, bf16[512,256]{1,0:T(8,128)(2,1)S(1)} %copy-done.2), kind=kOutput, calls=%fused_computation.1 | convolution fusion | flops 42123264 | bytes 1212416 | tf_op jit(solution)/shard_map/dot_general | solution.py:22
  (28 shorter events, 2.8 us)
Async XLA Ops:
  0.0 2.6 %copy-start = (bf16[1024,1024]{1,0:T(8,128)(2,1)S(1)}, bf16[1024,1024]{1,0:T(8,128)(2,1)}, u32[]{:S(2)}) copy-start(bf16[1024,1024]{1,0:T(8,128)(2,1)} %param.6) | copy-start | bytes 6291460
  0.0 4.2 %copy-start.1 = (bf16[512,256]{1,0:T(8,128)(2,1)S(1)}, bf16[512,256]{1,0:T(8,128)(2,1)}, u32[]{:S(2)}) copy-start(bf16[512,256]{1,0:T(8,128)(2,1)} %param.8) | copy-start | bytes 786436
  0.0 4.0 %copy-start.2 = (bf16[512,256]{1,0:T(8,128)(2,1)S(1)}, bf16[512,256]{1,0:T(8,128)(2,1)}, u32[]{:S(2)}) copy-start(bf16[512,256]{1,0:T(8,128)(2,1)} %param.9) | copy-start | bytes 786436
  1.5 2.7 %collective-permute-start = (bf16[64,256]{1,0:T(8,128)(2,1)S(1)}, bf16[64,256]{1,0:T(8,128)(2,1)S(1)}, u32[]{:S(2)}, u32[]{:S(2)}) collective-permute-start(bf16[64,256]{1,0:T(8,128)(2,1)S(1)} %convolution_convert_fusion), channel_id=1, source_target_pairs={{0,1},{1,0},{2,3},{3,2},{4,5},{5,4},{6,7},{7,6},{8,9},{9,8},{10,11... | collective-permute-start | bytes 98312 | tf_op jit(solution)/shard_map/ppermute | solution.py:14
  4.4 4.4 %collective-permute-start.1 = (bf16[64,256]{1,0:T(8,128)(2,1)S(1)}, bf16[64,256]{1,0:T(8,128)(2,1)S(1)}, u32[]{:S(2)}, u32[]{:S(2)}) collective-permute-start(bf16[64,256]{1,0:T(8,128)(2,1)S(1)} %fusion.6), channel_id=1, source_target_pairs={{0,2},{2,0},{1,3},{3,1},{4,6},{6,4},{5,7},{7,5},{8,10},{10,8},{9,1... | collective-permute-start | bytes 98312 | tf_op jit(solution)/shard_map/ppermute | solution.py:14
  8.9 2.8 %collective-permute-start.2 = (bf16[64,256]{1,0:T(8,128)(2,1)S(1)}, bf16[64,256]{1,0:T(8,128)(2,1)S(1)}, u32[]{:S(2)}, u32[]{:S(2)}) collective-permute-start(bf16[64,256]{1,0:T(8,128)(2,1)S(1)} %fusion.7), channel_id=1, source_target_pairs={{0,4},{4,0},{1,5},{5,1},{2,6},{6,2},{3,7},{7,3},{8,12},{12,8},{9,1... | collective-permute-start | bytes 98312 | tf_op jit(solution)/shard_map/ppermute | solution.py:14
  11.9 2.8 %collective-permute-start.3 = (bf16[64,256]{1,0:T(8,128)(2,1)S(1)}, bf16[64,256]{1,0:T(8,128)(2,1)S(1)}, u32[]{:S(2)}, u32[]{:S(2)}) collective-permute-start(bf16[64,256]{1,0:T(8,128)(2,1)S(1)} %fusion.8), channel_id=1, source_target_pairs={{0,8},{8,0},{1,9},{9,1},{2,10},{10,2},{3,11},{11,3},{4,12},{12,4},... | collective-permute-start | bytes 98312 | tf_op jit(solution)/shard_map/ppermute | solution.py:14
  14.9 3.7 %collective-permute-start.4 = (bf16[64,256]{1,0:T(8,128)(2,1)S(1)}, bf16[64,256]{1,0:T(8,128)(2,1)S(1)}, u32[]{:S(2)}, u32[]{:S(2)}) collective-permute-start(bf16[64,256]{1,0:T(8,128)(2,1)S(1)} %fusion.9), channel_id=1, source_target_pairs={{0,16},{16,0},{1,17},{17,1},{2,18},{18,2},{3,19},{19,3},{4,20},{20... | collective-permute-start | bytes 98312 | tf_op jit(solution)/shard_map/ppermute | solution.py:14
  17.2 25.1 %copy-start.3 = (bf16[1024,256]{1,0:T(8,128)(2,1)S(1)}, bf16[1024,256]{1,0:T(8,128)(2,1)}, u32[]{:S(2)}) copy-start(bf16[1024,256]{1,0:T(8,128)(2,1)} %param.7) | copy-start | bytes 1572868
  18.8 3.8 %collective-permute-start.5 = (bf16[64,256]{1,0:T(8,128)(2,1)S(1)}, bf16[64,256]{1,0:T(8,128)(2,1)S(1)}, u32[]{:S(2)}, u32[]{:S(2)}) collective-permute-start(bf16[64,256]{1,0:T(8,128)(2,1)S(1)} %fusion.10), channel_id=1, source_target_pairs={{0,16},{16,0},{1,17},{17,1},{2,18},{18,2},{3,19},{19,3},{4,20},{20... | collective-permute-start | bytes 98312 | tf_op jit(solution)/shard_map/ppermute | solution.py:14
  22.9 3.0 %collective-permute-start.6 = (bf16[64,256]{1,0:T(8,128)(2,1)S(1)}, bf16[64,256]{1,0:T(8,128)(2,1)S(1)}, u32[]{:S(2)}, u32[]{:S(2)}) collective-permute-start(bf16[64,256]{1,0:T(8,128)(2,1)S(1)} %fusion.11), channel_id=1, source_target_pairs={{0,8},{8,0},{1,9},{9,1},{2,10},{10,2},{3,11},{11,3},{4,12},{12,4},... | collective-permute-start | bytes 98312 | tf_op jit(solution)/shard_map/ppermute | solution.py:14
  26.2 2.8 %collective-permute-start.7 = (bf16[64,256]{1,0:T(8,128)(2,1)S(1)}, bf16[64,256]{1,0:T(8,128)(2,1)S(1)}, u32[]{:S(2)}, u32[]{:S(2)}) collective-permute-start(bf16[64,256]{1,0:T(8,128)(2,1)S(1)} %fusion.12), channel_id=1, source_target_pairs={{0,4},{4,0},{1,5},{5,1},{2,6},{6,2},{3,7},{7,3},{8,12},{12,8},{9,1... | collective-permute-start | bytes 98312 | tf_op jit(solution)/shard_map/ppermute | solution.py:14
  29.3 2.8 %collective-permute-start.8 = (bf16[64,256]{1,0:T(8,128)(2,1)S(1)}, bf16[64,256]{1,0:T(8,128)(2,1)S(1)}, u32[]{:S(2)}, u32[]{:S(2)}) collective-permute-start(bf16[64,256]{1,0:T(8,128)(2,1)S(1)} %fusion.13), channel_id=1, source_target_pairs={{0,2},{2,0},{1,3},{3,1},{4,6},{6,4},{5,7},{7,5},{8,10},{10,8},{9,1... | collective-permute-start | bytes 98312 | tf_op jit(solution)/shard_map/ppermute | solution.py:14
  32.5 9.7 %collective-permute-start.9 = (bf16[64,256]{1,0:T(8,128)(2,1)S(1)}, bf16[64,256]{1,0:T(8,128)(2,1)S(1)}, u32[]{:S(2)}, u32[]{:S(2)}) collective-permute-start(bf16[64,256]{1,0:T(8,128)(2,1)S(1)} %fusion.14), channel_id=1, source_target_pairs={{0,1},{1,0},{2,3},{3,2},{4,5},{5,4},{6,7},{7,6},{8,9},{9,8},{10,11... | collective-permute-start | bytes 98312 | tf_op jit(solution)/shard_map/ppermute | solution.py:14
where the time goes:
time: 43.8 us; the launch traced here: 43.3 us
  starting transfers between devices  22.3 us (51%)
  waiting for transfers between devices  11.7 us (27%)
  matrix products  9.19 us (21%)
    ppermute x10, starting transfers between devices, from_partner(): return lax.ppermute(block, axis, route)  22.3 us
    ppermute x10, waiting for transfers between devices, from_partner(): return lax.ppermute(block, axis, route)  11.7 us
    dot_general x21, matrix products, times_matrix(): return jnp.dot(values, matrix, preferred_element_type=jnp.float32)  6.64 us
    dot_general x11, matrix products, times_transposed(): lax.dot_general(values, matrix, (((1,), (1,)), ((), ())), preferred_eleme...  2.55 us
  transfers between devices with their start and end apart: 10, of which 9 were waited for; matrix products, arithmetic and copies ran while one was open for 10% of the time, Pallas kernels for 0%

commit v1 on v0

v1 whole, which is shorter than its diff:
```python
import functools

import jax
import jax.numpy as jnp
from jax import lax
from jax.experimental import pallas as pl
from jax.experimental.pallas import tpu as pltpu
from jax.sharding import PartitionSpec as P

MESH = pl.DeviceIdType.MESH


def times_matrix(values, matrix):
    return jnp.dot(values, matrix, preferred_element_type=jnp.float32)


def times_transposed(values, matrix):
    return lax.dot_general(
        values, matrix, (((1,), (1,)), ((), ())), preferred_element_type=jnp.float32
    )


def partner_of(me, level):
    bit = 1 << (level - 1)
    return me + bit - 2 * bit * (lax.div(me, bit) % 2)


def kernel(
    levels,
    sides_hbm,
    inverse_hbm,
    basis_hbm,
    transfer_hbm,
    coupling_hbm,
    out_ref,
    sides,
    inverse,
    basis,
    transfer,
    coupling,
    own_t,
    far_t,
    own_h,
    far_h,
    direct,
    near,
    load_sem,
    up_send,
    up_recv,
    down_send,
    down_recv,
):
    me = lax.axis_index("leaf")
    rank = basis.shape[1]
    points = sides.shape[1]
    loads = [
        pltpu.make_async_copy(src, dst, load_sem.at[k])
        for k, (src, dst) in enumerate(
            (
                (sides_hbm, sides),
                (basis_hbm, basis),
                (transfer_hbm, transfer),
                (coupling_hbm, coupling),
                (inverse_hbm, inverse),
            )
        )
    ]
    for load in loads:
        load.start()
    barrier = pltpu.get_barrier_semaphore()
    for level in range(1, levels + 1):
        pl.semaphore_signal(
            barrier, inc=1, device_id=(partner_of(me, level),), device_id_type=MESH
        )

    def exchange(src, dst, send, recv, level):
        copy = pltpu.make_async_remote_copy(
            src_ref=src.at[level - 1],
            dst_ref=dst.at[level - 1],
            send_sem=send.at[level - 1],
            recv_sem=recv.at[level - 1],
            device_id=(partner_of(me, level),),
            device_id_type=MESH,
        )
        copy.start()
        return copy

    loads[0].wait()
    loads[1].wait()
    own_t[0] = times_matrix(sides[...], basis[...]).astype(jnp.bfloat16)
    pl.semaphore_wait(barrier, levels)

    width = points // levels // 128 * 128
    pieces = [(k * width, width) for k in range(levels)]
    pieces[-1] = ((levels - 1) * width, points - (levels - 1) * width)
    copies = []
    for level in range(1, levels + 1):
        copy = exchange(own_t, far_t, up_send, up_recv, level)
        copies.append(copy)
        if level == 1:
            loads[2].wait()
        mine = own_t[level - 1]
        partial = times_matrix(mine, transfer[:rank])
        if level == 2:
            loads[3].wait()
        if level >= 2:
            near[level - 2] = times_matrix(far_t[level - 2], coupling[:rank]) + times_matrix(
                own_t[level - 2], coupling[rank:]
            )
        copy.wait_recv()
        total = partial + times_matrix(far_t[level - 1], transfer[rank:])
        if level < levels:
            own_t[level] = total.astype(jnp.bfloat16)
        else:
            own_h[level - 1] = total.astype(jnp.bfloat16)
    for level in range(levels, 0, -1):
        copy = exchange(own_h, far_h, down_send, down_recv, level)
        copies.append(copy)
        partial = times_transposed(own_h[level - 1], transfer[:rank])
        if level == levels:
            near[level - 1] = times_matrix(far_t[level - 1], coupling[:rank]) + times_matrix(
                own_t[level - 1], coupling[rank:]
            )
            loads[4].wait()
        partial = partial + near[level - 1]
        start, size = pieces[level - 1]
        if size:
            direct[:, start : start + size] = times_matrix(
                sides[...], inverse[:, start : start + size]
            )
        copy.wait_recv()
        total = partial + times_transposed(far_h[level - 1], transfer[rank:])
        if level > 1:
            own_h[level - 2] = total.astype(jnp.bfloat16)
    node_h = total.astype(jnp.bfloat16)
    out_ref[...] = (direct[...] + times_transposed(node_h, basis[...])).astype(jnp.bfloat16)
    for copy in copies:
        copy.wait_send()


def body(right_sides, leaf_inverse, leaf_basis, transfer, coupling):
    levels = lax.axis_size("leaf").bit_length() - 1
    columns = right_sides.shape[0]
    rank = leaf_basis.shape[1]
    steps = pltpu.VMEM((levels, columns, rank), jnp.bfloat16)
    args = (right_sides, leaf_inverse, leaf_basis, transfer, coupling)
    return pl.pallas_call(
        functools.partial(kernel, levels),
        out_shape=jax.ShapeDtypeStruct(right_sides.shape, jnp.bfloat16),
        in_specs=[pl.BlockSpec(memory_space=pl.ANY)] * len(args),
        out_specs=pl.BlockSpec(memory_space=pltpu.VMEM),
        scratch_shapes=[pltpu.VMEM(a.shape, a.dtype) for a in args]
        + [steps] * 4
        + [
            pltpu.VMEM(right_sides.shape, jnp.float32),
            pltpu.VMEM((levels, columns, rank), jnp.float32),
            pltpu.SemaphoreType.DMA((len(args),)),
        ]
        + [pltpu.SemaphoreType.DMA((levels,))] * 4,
        compiler_params=pltpu.CompilerParams(
            collective_id=0, has_side_effects=True, vmem_limit_bytes=32 << 20
        ),
    )(*args)


def solution(mesh):
    placed = (P(None, "leaf"), P("leaf", None), P("leaf", None), P("leaf", None), P("leaf", None))
    return jax.shard_map(
        body, mesh=mesh, in_specs=placed, out_specs=P(None, "leaf"), check_vma=False
    )
```

time: 43.8 us -> 38.7 us (0.88)
  Pallas kernels: 0 us -> 32.3 us
  starting transfers between devices: 22.3 us -> 0 us
  waiting for transfers between devices: 11.7 us -> 0 us
  matrix products: 9.19 us -> 0 us
  local copies, waits for them, and re-layouts: 0.06 us -> 6.09 us
    pallas_call x0 -> x1, Pallas kernels: none -> 32.3 us  [body(): pl.pallas_call(functools.partial(kernel, levels), out_shape=jax.ShapeDtyp...]
    ppermute x10 -> x0, starting transfers between devices: 22.3 us -> none  [from_partner(): return lax.ppermute(block, axis, route)]
    ppermute x10 -> x0, waiting for transfers between devices: 11.7 us -> none  [from_partner(): return lax.ppermute(block, axis, route)]
    dot_general x32 -> x0, matrix products: 9.19 us -> none  [the longest x21 6.64 us: times_matrix(): return jnp.dot(values, matrix, preferred_element_type=jnp.float32)]
    unnamed x8 -> x11, local copies, waits for them, and re-layouts: 0.06 us -> 6.09 us
  transfers between devices with their start and end apart: 10 -> 0, of which waited for: 9 -> 0; matrix products, arithmetic and copies ran while one was open for 10% -> 0% of each run, Pallas kernels for 0% -> 0%
where the time goes in v1:
time: 38.7 us; the launch traced here: 38.4 us
  Pallas kernels  32.3 us (83%)
  local copies, waits for them, and re-layouts  6.09 us (16%)
    pallas_call x1, Pallas kernels, body(): pl.pallas_call(functools.partial(kernel, levels), out_shape=jax.ShapeDtyp...  32.3 us
    unnamed x11, local copies, waits for them, and re-layouts  6.09 us

profile of v1, /device:TPU:1, one launch (start us, length us, event | category | flops | bytes accessed | tf_op | source)
XLA Modules:
  0.0 38.4 jit_solution(5419027025300676735)
XLA Ops:
  0.0 0.0 copy-start
  0.0 1.6 %copy-done = bf16[1024,1024]{1,0:T(8,128)(2,1)S(1)} copy-done((bf16[1024,1024]{1,0:T(8,128)(2,1)S(1)}, bf16[1024,1024]{1,0:T(8,128)(2,1)}, u32[]{:S(2)}) %copy-start) | copy-done | bytes 2097176
  1.6 0.0 copy-start.1
  1.6 1.0 %copy-done.1 = bf16[1024,256]{1,0:T(8,128)(2,1)S(1)} copy-done((bf16[1024,256]{1,0:T(8,128)(2,1)S(1)}, bf16[1024,256]{1,0:T(8,128)(2,1)}, u32[]{:S(2)}) %copy-start.1) | copy-done | bytes 524312
  2.6 0.0 copy-start.2
  2.6 0.9 %copy-done.2 = bf16[512,256]{1,0:T(8,128)(2,1)S(1)} copy-done((bf16[512,256]{1,0:T(8,128)(2,1)S(1)}, bf16[512,256]{1,0:T(8,128)(2,1)}, u32[]{:S(2)}) %copy-start.2) | copy-done | bytes 262168
  3.6 0.0 copy-start.3
  3.6 0.9 %copy-done.3 = bf16[512,256]{1,0:T(8,128)(2,1)S(1)} copy-done((bf16[512,256]{1,0:T(8,128)(2,1)S(1)}, bf16[512,256]{1,0:T(8,128)(2,1)}, u32[]{:S(2)}) %copy-start.3) | copy-done | bytes 262168
  4.5 0.0 copy-start.4
  4.5 0.9 %copy-done.4 = bf16[64,1024]{1,0:T(8,128)(2,1)S(1)} copy-done((bf16[64,1024]{1,0:T(8,128)(2,1)S(1)}, bf16[64,1024]{1,0:T(8,128)(2,1)}, u32[]{:S(2)}) %copy-start.4) | copy-done | bytes 131096
  5.4 32.3 %shard_map.55 = bf16[64,1024]{1,0:T(8,128)(2,1)S(1)} custom-call(bf16[64,1024]{1,0:T(8,128)(2,1)S(1)} %copy-done.4, bf16[1024,1024]{1,0:T(8,128)(2,1)S(1)} %copy-done, bf16[1024,256]{1,0:T(8,128)(2,1)S(1)} %copy-done.1, bf16[512,256]{1,0:T(8,128)(2,1)S(1)} %copy-done.2, bf16[512,256]{1,0:T(8,128)(2,1)S(1)} %copy-done.3), custom_call_target="tpu_custom_call" | custom-call | tf_op jit(solution)/shard_map/pallas_call | solution.py:147
  37.8 0.7 %copy.7 = bf16[64,1024]{1,0:T(8,128)(2,1)} copy(bf16[64,1024]{1,0:T(8,128)(2,1)S(1)} %shard_map.55) | data formatting | bytes 262144
Async XLA Ops:
  0.0 1.6 %copy-start = (bf16[1024,1024]{1,0:T(8,128)(2,1)S(1)}, bf16[1024,1024]{1,0:T(8,128)(2,1)}, u32[]{:S(2)}) copy-start(bf16[1024,1024]{1,0:T(8,128)(2,1)} %inverse_hbm.1) | copy-start | bytes 6291460
  1.6 1.0 %copy-start.1 = (bf16[1024,256]{1,0:T(8,128)(2,1)S(1)}, bf16[1024,256]{1,0:T(8,128)(2,1)}, u32[]{:S(2)}) copy-start(bf16[1024,256]{1,0:T(8,128)(2,1)} %basis_hbm.1) | copy-start | bytes 1572868
  2.6 0.9 %copy-start.2 = (bf16[512,256]{1,0:T(8,128)(2,1)S(1)}, bf16[512,256]{1,0:T(8,128)(2,1)}, u32[]{:S(2)}) copy-start(bf16[512,256]{1,0:T(8,128)(2,1)} %transfer_hbm.1) | copy-start | bytes 786436
  3.6 0.9 %copy-start.3 = (bf16[512,256]{1,0:T(8,128)(2,1)S(1)}, bf16[512,256]{1,0:T(8,128)(2,1)}, u32[]{:S(2)}) copy-start(bf16[512,256]{1,0:T(8,128)(2,1)} %coupling_hbm.1) | copy-start | bytes 786436
  4.5 0.9 %copy-start.4 = (bf16[64,1024]{1,0:T(8,128)(2,1)S(1)}, bf16[64,1024]{1,0:T(8,128)(2,1)}, u32[]{:S(2)}) copy-start(bf16[64,1024]{1,0:T(8,128)(2,1)} %sides_hbm.1) | copy-start | bytes 393220

commit v2 on v1

--- a/solution.py
+++ b/solution.py
@@ -158,7 +158,7 @@
         ]
         + [pltpu.SemaphoreType.DMA((levels,))] * 4,
         compiler_params=pltpu.CompilerParams(
-            collective_id=0, has_side_effects=True, vmem_limit_bytes=32 << 20
+            collective_id=0, has_side_effects=True, vmem_limit_bytes=60 << 20
         ),
     )(*args)
 

time: 38.7 us -> 34.1 us (0.88)
  local copies, waits for them, and re-layouts: 6.09 us -> 1.57 us
    unnamed x11 -> x1, local copies, waits for them, and re-layouts: 6.09 us -> 1.57 us
where the time goes in v2:
time: 34.1 us; the launch traced here: 33.9 us
  Pallas kernels  32.4 us (95%)
  local copies, waits for them, and re-layouts  1.57 us (5%)
    pallas_call x1, Pallas kernels, body(): pl.pallas_call(functools.partial(kernel, levels), out_shape=jax.ShapeDtyp...  32.4 us
    unnamed x1, local copies, waits for them, and re-layouts  1.57 us

profile of v2, /device:TPU:1, one launch (start us, length us, event | category | flops | bytes accessed | tf_op | source)
XLA Modules:
  0.0 33.9 jit_solution(11542994389478230503)
XLA Ops:
  0.0 32.4 %shard_map.55 = bf16[64,1024]{1,0:T(8,128)(2,1)} custom-call(bf16[64,1024]{1,0:T(8,128)(2,1)} %sides_hbm.1, bf16[1024,1024]{1,0:T(8,128)(2,1)} %inverse_hbm.1, bf16[1024,256]{1,0:T(8,128)(2,1)} %basis_hbm.1, bf16[512,256]{1,0:T(8,128)(2,1)} %transfer_hbm.1, bf16[512,256]{1,0:T(8,128)(2,1)} %coupling_hbm.1), custom_call_target="tpu_custom_call" | custom-call | tf_op jit(solution)/shard_map/pallas_call | solution.py:147
  32.4 1.6 %copy.7 = bf16[64,1024]{1,0:T(8,128)(2,1)} copy(bf16[64,1024]{1,0:T(8,128)(2,1)} %shard_map.55) | data formatting | bytes 262144

commit v3 on v2

v3 whole, which is shorter than its diff:
```python
import functools

import jax
import jax.numpy as jnp
from jax import lax
from jax.experimental import pallas as pl
from jax.experimental.pallas import tpu as pltpu
from jax.sharding import PartitionSpec as P

MESH = pl.DeviceIdType.MESH


def times_matrix(values, matrix):
    return jnp.dot(values, matrix, preferred_element_type=jnp.float32)


def times_transposed(values, matrix):
    return lax.dot_general(
        values, matrix, (((1,), (1,)), ((), ())), preferred_element_type=jnp.float32
    )


def rounded(values):
    return values.astype(jnp.bfloat16)


def flipped(me, levels):
    for level in levels:
        bit = 1 << (level - 1)
        me = me + bit - 2 * bit * (lax.div(me, bit) % 2)
    return me


def rounds(levels):
    up = [(level,) for level in range(1, min(levels, 2) + 1)]
    up += [(low, low + 1) if low < levels else (low,) for low in range(3, levels + 1, 2)]
    return up, [(level,) for level in range(levels, 0, -1)]


def count_messages(up, down):
    return sum(3 if len(r) == 2 else 1 for r in up) + sum(4 if len(r) == 2 else 1 for r in down)


def kernel(
    levels,
    sides_hbm,
    inverse_hbm,
    basis_hbm,
    transfer_hbm,
    coupling_hbm,
    out_ref,
    sides,
    inverse,
    basis,
    transfer,
    coupling,
    maps,
    turned,
    own_t,
    far_t,
    own_h,
    near,
    near_out,
    inbox,
    direct,
    load_sem,
    send_sem,
    recv_sem,
    maps_send,
    maps_recv,
):
    me = lax.axis_index("leaf")
    rank = basis.shape[1]
    up, down = rounds(levels)
    loads = [
        pltpu.make_async_copy(src, dst, load_sem.at[k])
        for k, (src, dst) in enumerate(
            (
                (sides_hbm, sides),
                (basis_hbm, basis),
                (transfer_hbm, transfer),
                (coupling_hbm, coupling),
                (inverse_hbm, inverse),
            )
        )
    ]
    for load in loads:
        load.start()
    peers = sorted({(level,) for level in range(1, levels + 1)} | {
        tuple(sorted(r)) for r in up + down if len(r) == 2
    })
    barrier = pltpu.get_barrier_semaphore()
    for peer in peers:
        pl.semaphore_signal(barrier, inc=1, device_id=(flipped(me, peer),), device_id_type=MESH)

    sent = []
    slots = iter(range(count_messages(up, down)))

    def post(src, peer):
        slot = next(slots)
        copy = pltpu.make_async_remote_copy(
            src_ref=src,
            dst_ref=inbox.at[slot],
            send_sem=send_sem.at[slot],
            recv_sem=recv_sem.at[slot],
            device_id=(flipped(me, peer),),
            device_id_type=MESH,
        )
        copy.start()
        sent.append(copy)
        return copy, inbox.at[slot]

    def take(message):
        message[0].wait_recv()
        return message[1][...]

    maps_copy = {}

    def post_maps(level):
        index = level // 2 - 1
        copy = pltpu.make_async_remote_copy(
            src_ref=transfer,
            dst_ref=maps.at[index],
            send_sem=maps_send.at[index],
            recv_sem=maps_recv.at[index],
            device_id=(flipped(me, (level,)),),
            device_id_type=MESH,
        )
        copy.start()
        sent.append(copy)
        maps_copy[level] = [copy, False]

    def maps_of(level):
        entry = maps_copy[level]
        if not entry[1]:
            entry[0].wait_recv()
            entry[1] = True
        return maps.at[level // 2 - 1]

    loads[0].wait()
    loads[1].wait()
    own_t[0] = rounded(times_matrix(sides[...], basis[...]))
    loads[2].wait()
    pl.semaphore_wait(barrier, len(peers))

    near_in = {}
    later = []

    def idle():
        while later:
            later.pop(0)()

    def add_near(level):
        def run():
            near[level - 1] = times_matrix(far_t[level - 1], coupling[:rank]) + times_matrix(
                own_t[level - 1], coupling[rank:]
            )
            for high, *low in down:
                if low and high == level:
                    near_out[level - 1] = rounded(near[level - 1])
                    near_in[level] = post(near_out.at[level - 1], tuple(low))

        later.append(run)

    def keep(level, values):
        if level < levels:
            own_t[level] = values
        else:
            own_h[levels - 1] = values

    def turn(index, source):
        for half in (slice(0, rank), slice(rank, 2 * rank)):
            turned[index, half] = source[half].T

    def add_direct():
        loads[4].wait()
        direct[...] = times_matrix(sides[...], inverse[...])

    for group in up:
        low, high = group[0], group[-1]
        mine = own_t.at[low - 1]
        if len(group) == 2:
            both = post(mine, group)
        first = post(mine, (low,))
        if len(group) == 2:
            second = post(mine, (high,))
        if low == 1:
            for level in range(4, levels + 1, 2):
                post_maps(level)
            loads[3].wait()
        if low == 2:
            later.append(lambda: turn(0, transfer))
            later.append(add_direct)
        partial = times_matrix(mine[...], transfer[:rank])
        idle()
        far_t[low - 1] = take(first)
        total = rounded(partial + times_matrix(far_t[low - 1], transfer[rank:]))
        keep(low, total)
        add_near(low)
        if len(group) == 2:
            theirs = maps_of(high)
            partial = times_matrix(total, transfer[:rank])
            other = times_matrix(take(second), theirs[:rank])
            other = rounded(other + times_matrix(take(both), theirs[rank:]))
            far_t[high - 1] = other
            keep(high, rounded(partial + times_matrix(other, transfer[rank:])))
            add_near(high)

    for group in down:
        high, low = group[0], group[-1]
        mine = own_h.at[high - 1]
        if len(group) == 2:
            both = post(mine, group)
        first = post(mine, (high,))
        if len(group) == 2:
            second = post(mine, (low,))
        partial = times_matrix(mine[...], turned[0, :rank])
        idle()
        partial = partial + near[high - 1]
        if len(group) == 2:
            other = times_matrix(take(second), turned[low // 2, :rank])
            other = other + take(near_in[high]).astype(jnp.float32)
        total = rounded(
            partial + times_matrix(take(first), turned[0, rank:])
        )
        if len(group) == 2:
            partial = times_matrix(total, turned[0, :rank]) + near[low - 1]
            other = rounded(other + times_matrix(take(both), turned[low // 2, rank:]))
            total = rounded(partial + times_matrix(other, turned[0, rank:]))
        if low > 1:
            own_h[low - 2] = total
    if levels < 2:
        add_direct()
    out_ref[...] = rounded(direct[...] + times_transposed(total, basis[...]))
    for copy in sent:
        copy.wait_send()


def body(right_sides, leaf_inverse, leaf_basis, transfer, coupling):
    levels = lax.axis_size("leaf").bit_length() - 1
    columns = right_sides.shape[0]
    rank = leaf_basis.shape[1]
    messages = count_messages(*rounds(levels))
    shared = max(levels // 2, 1)
    steps = pltpu.VMEM((levels, columns, rank), jnp.bfloat16)
    args = (right_sides, leaf_inverse, leaf_basis, transfer, coupling)
    return pl.pallas_call(
        functools.partial(kernel, levels),
        out_shape=jax.ShapeDtypeStruct(right_sides.shape, jnp.bfloat16),
        in_specs=[pl.BlockSpec(memory_space=pl.ANY)] * len(args),
        out_specs=pl.BlockSpec(memory_space=pltpu.VMEM),
        scratch_shapes=[pltpu.VMEM(a.shape, a.dtype) for a in args]
        + [pltpu.VMEM((shared,) + transfer.shape, jnp.bfloat16)]
        + [pltpu.VMEM((shared + 1,) + transfer.shape, jnp.bfloat16)]
        + [steps] * 3
        + [
            pltpu.VMEM((levels, columns, rank), jnp.float32),
            steps,
            pltpu.VMEM((messages, columns, rank), jnp.bfloat16),
            pltpu.VMEM(right_sides.shape, jnp.float32),
            pltpu.SemaphoreType.DMA((len(args),)),
            pltpu.SemaphoreType.DMA((messages,)),
            pltpu.SemaphoreType.DMA((messages,)),
            pltpu.SemaphoreType.DMA((shared,)),
            pltpu.SemaphoreType.DMA((shared,)),
        ],
        compiler_params=pltpu.CompilerParams(
            collective_id=0, has_side_effects=True, vmem_limit_bytes=60 << 20
        ),
    )(*args)


def solution(mesh):
    placed = (P(None, "leaf"), P("leaf", None), P("leaf", None), P("leaf", None), P("leaf", None))
    return jax.shard_map(
        body, mesh=mesh, in_specs=placed, out_specs=P(None, "leaf"), check_vma=False
    )
```

time: 34.1 us -> 33.9 us (level)
  no operation moved by 1% of the time
where the time goes in v3:
time: 33.9 us; the launch traced here: 33.7 us
  Pallas kernels  32.2 us (95%)
  local copies, waits for them, and re-layouts  1.57 us (5%)
    pallas_call x1, Pallas kernels, body(): pl.pallas_call(functools.partial(kernel, levels), out_shape=jax.ShapeDtyp...  32.2 us
    unnamed x1, local copies, waits for them, and re-layouts  1.57 us

profile of v3, /device:TPU:1, one launch (start us, length us, event | category | flops | bytes accessed | tf_op | source)
XLA Modules:
  0.0 33.7 jit_solution(17019203495121978658)
XLA Ops:
  0.0 32.2 %shard_map.55 = bf16[64,1024]{1,0:T(8,128)(2,1)} custom-call(bf16[64,1024]{1,0:T(8,128)(2,1)} %sides_hbm.1, bf16[1024,1024]{1,0:T(8,128)(2,1)} %inverse_hbm.1, bf16[1024,256]{1,0:T(8,128)(2,1)} %basis_hbm.1, bf16[512,256]{1,0:T(8,128)(2,1)} %transfer_hbm.1, bf16[512,256]{1,0:T(8,128)(2,1)} %coupling_hbm.1), custom_call_target="tpu_custom_call" | custom-call | tf_op jit(solution)/shard_map/pallas_call | solution.py:247
  32.2 1.6 %copy.7 = bf16[64,1024]{1,0:T(8,128)(2,1)} copy(bf16[64,1024]{1,0:T(8,128)(2,1)} %shard_map.55) | data formatting | bytes 262144

commit v4 on v3

--- a/solution.py
+++ b/solution.py
@@ -118,22 +118,27 @@
 
     def post_maps(level):
         index = level // 2 - 1
-        copy = pltpu.make_async_remote_copy(
-            src_ref=transfer,
-            dst_ref=maps.at[index],
-            send_sem=maps_send.at[index],
-            recv_sem=maps_recv.at[index],
-            device_id=(flipped(me, (level,)),),
-            device_id_type=MESH,
-        )
-        copy.start()
-        sent.append(copy)
-        maps_copy[level] = [copy, False]
+        copies = []
+        for half in range(2):
+            rows = pl.ds(half * rank, rank)
+            copy = pltpu.make_async_remote_copy(
+                src_ref=transfer.at[rows],
+                dst_ref=maps.at[index, rows],
+                send_sem=maps_send.at[index, half],
+                recv_sem=maps_recv.at[index, half],
+                device_id=(flipped(me, (level,)),),
+                device_id_type=MESH,
+            )
+            copy.start()
+            copies.append(copy)
+            sent.append(copy)
+        maps_copy[level] = [copies, False]
 
     def maps_of(level):
         entry = maps_copy[level]
         if not entry[1]:
-            entry[0].wait_recv()
+            for copy in entry[0]:
+                copy.wait_recv()
             entry[1] = True
         return maps.at[level // 2 - 1]
 
@@ -261,8 +266,8 @@
             pltpu.SemaphoreType.DMA((len(args),)),
             pltpu.SemaphoreType.DMA((messages,)),
             pltpu.SemaphoreType.DMA((messages,)),
-            pltpu.SemaphoreType.DMA((shared,)),
-            pltpu.SemaphoreType.DMA((shared,)),
+            pltpu.SemaphoreType.DMA((shared, 2)),
+            pltpu.SemaphoreType.DMA((shared, 2)),
         ],
         compiler_params=pltpu.CompilerParams(
             collective_id=0, has_side_effects=True, vmem_limit_bytes=60 << 20

time: 33.9 us -> 33.9 us (level)
  no operation moved by 1% of the time
where the time goes in v4:
time: 33.9 us; the launch traced here: 33.8 us
  Pallas kernels  32.2 us (95%)
  local copies, waits for them, and re-layouts  1.57 us (5%)
    pallas_call x1, Pallas kernels, body(): pl.pallas_call(functools.partial(kernel, levels), out_shape=jax.ShapeDtyp...  32.2 us
    unnamed x1, local copies, waits for them, and re-layouts  1.57 us

profile of v4, /device:TPU:1, one launch (start us, length us, event | category | flops | bytes accessed | tf_op | source)
XLA Modules:
  0.0 33.8 jit_solution(6528657036250751660)
XLA Ops:
  0.0 32.2 %shard_map.55 = bf16[64,1024]{1,0:T(8,128)(2,1)} custom-call(bf16[64,1024]{1,0:T(8,128)(2,1)} %sides_hbm.1, bf16[1024,1024]{1,0:T(8,128)(2,1)} %inverse_hbm.1, bf16[1024,256]{1,0:T(8,128)(2,1)} %basis_hbm.1, bf16[512,256]{1,0:T(8,128)(2,1)} %transfer_hbm.1, bf16[512,256]{1,0:T(8,128)(2,1)} %coupling_hbm.1), custom_call_target="tpu_custom_call" | custom-call | tf_op jit(solution)/shard_map/pallas_call | solution.py:252
  32.2 1.6 %copy.7 = bf16[64,1024]{1,0:T(8,128)(2,1)} copy(bf16[64,1024]{1,0:T(8,128)(2,1)} %shard_map.55) | data formatting | bytes 262144
